TPU v7x, 32 devices: a whole 2x2x4 slice. The times are simulated.
32 devices in a mesh: parts: 2 (over x), chan: 16 (over z, y, core).
Axes of the slice: x: 2, y: 2, z: 4, core: 2. Of those that a mesh axis runs over, the one named last changes fastest.
Arguments:
- spectra: bfloat16 [2, 256, 2, 2048], P(None, ('parts', 'chan')), parts along dimension 1, may hold values from -600 to 600
- pair_blocks: int32 [512, 2], P(('parts', 'chan')), parts along dimension 0, may hold values from 0 to 31, as said below
- pair_dest: int32 [512, 2], P(('parts', 'chan')), parts along dimension 0, may hold values from 0 to 15, as said below
- pair_count: int32 [32], P(('parts', 'chan')), parts along dimension 0, may hold values from 1 to 16, as said below
Outputs:
- stacks: float32 [512, 16, 4096], P(('parts', 'chan')), parts along dimension 0
There are 2 independent parts, one for each index of `parts`. A program takes and returns all parts, laid end to end along the dimension named above; each array names one. Nothing has to cross between parts.
Inputs may be any that keep to these rules, and one draw needn't show every extreme that they name: `pair_blocks`: every row r names a first block a with (r div 16) * 2 <= a < (r div 16 + 1) * 2, and a second block b with |a - b| <= 2; that distance occurs in a used row. `pair_dest`: the used rows of one device name distinct owners; no two used rows name the same owner and slot; some owner receives a used row from every device. `pair_count`: some device uses all 16 of its rows.
All inputs are finite; a program needn't handle non-finite values.
Results may differ from a plain program's by a relative error of at most 0.0057.
Values may be sent and summed in bfloat16 or wider, within the bound.
A program may use at most 640 MiB of HBM per device.

v0:
```python
import math

import jax
import jax.numpy as jnp
from jax import lax
from jax.sharding import PartitionSpec as P

LAGS = 4096
FREQ = 2048
CH = 4


def with_halo(cells, sides, width):
    for axis, dim in sides:
        count = lax.axis_size(axis)
        ends = count - 1
        head = lax.slice_in_dim(cells, 0, width, axis=dim)
        tail = lax.slice_in_dim(cells, cells.shape[dim] - width, cells.shape[dim], axis=dim)
        cells = jnp.concatenate(
            [
                lax.ppermute(tail, axis, [(i, (i + 1) % count) for i in range(ends)]),
                cells,
                lax.ppermute(head, axis, [((i + 1) % count, i) for i in range(ends)]),
            ],
            axis=dim,
        )
    return cells


def make_basis(bin_count, lags):
    freq_bins = jnp.arange(bin_count, dtype=jnp.int32)
    delays = jnp.arange(lags, dtype=jnp.int32)
    quarter = jnp.arange(2, dtype=jnp.int32) * (lags // 4)
    phase_index = (freq_bins[None, :, None] * delays[None, None, :] + quarter[:, None, None]) % lags
    angles = phase_index.astype(jnp.float32) * (2.0 * math.pi / lags)
    weight = jnp.where(freq_bins == 0, 1.0, 2.0).astype(jnp.float32)[None, :, None] / (
        2.0 * math.sqrt(bin_count)
    )
    return (weight * jnp.cos(angles)).astype(jnp.bfloat16).reshape(2 * bin_count, lags)


def whiten(spectra):
    values = spectra.astype(jnp.float32)
    mean_power = jnp.mean(values * values, axis=(2, 3), keepdims=True)
    return (values / jnp.sqrt(mean_power + 1e-06)).astype(jnp.bfloat16)


def cross_rows(whitened, blocks, weights):
    segments, channels, two_sides, bin_count = whitened.shape
    block_total = channels // CH
    row_total = blocks.shape[0]
    grouped = whitened.reshape(segments, block_total, CH * two_sides * bin_count)
    block_ids = jnp.arange(block_total, dtype=jnp.int32)

    def select(column):
        one_hot = (blocks[:, column][:, None] == block_ids[None, :]).astype(jnp.bfloat16)
        picked = jnp.einsum("rb,sbx->srx", one_hot, grouped, preferred_element_type=jnp.float32)
        return picked.astype(jnp.bfloat16).reshape(segments, row_total, CH, two_sides, bin_count)

    first_side = select(0)
    second_side = select(1)
    rotated = jnp.stack([-second_side[:, :, :, 1, :], second_side[:, :, :, 0, :]], axis=3)
    both_sides = jnp.stack([second_side, rotated], axis=3)
    stacked = jnp.einsum(
        "sripf,srjcpf->rijcf", first_side, both_sides, preferred_element_type=jnp.float32
    )
    row_scale = weights.astype(jnp.float32) / segments
    stacked = stacked * row_scale[:, None, None, None, None]
    return stacked.astype(jnp.bfloat16).reshape(row_total * CH * CH, two_sides * bin_count)


def sending_plan(pair_dest, pair_count, dev_count):
    slot_count = pair_dest.shape[0]
    positions = jnp.arange(slot_count, dtype=jnp.int32)
    in_use = positions < pair_count[0]
    matches = in_use[None, :] & (
        pair_dest[None, :, 0] == jnp.arange(dev_count, dtype=jnp.int32)[:, None]
    )
    present = jnp.any(matches, axis=1)
    chosen = jnp.sum(jnp.where(matches, positions[None, :], 0), axis=1)
    return (in_use, present, chosen)


def receiving_plan(all_dest, all_count, own_index, slot_count):
    row_count = all_dest.shape[0]
    dev_count = row_count // slot_count
    row_ids = jnp.arange(row_count, dtype=jnp.int32)
    in_use = row_ids % slot_count < all_count[row_ids // slot_count]
    mine = in_use & (all_dest[:, 0] == own_index)
    from_slot = jnp.max(jnp.where(mine, all_dest[:, 1], -1).reshape(dev_count, slot_count), axis=1)
    matches = from_slot[None, :] == jnp.arange(slot_count, dtype=jnp.int32)[:, None]
    filled = jnp.any(matches, axis=1)
    source = jnp.sum(jnp.where(matches, jnp.arange(dev_count, dtype=jnp.int32)[None, :], 0), axis=1)
    return (filled, source)


def shards(spectra, pair_blocks, pair_dest, pair_count):
    slot_count = pair_dest.shape[0]
    dev_count = lax.axis_size("chan")
    own_index = lax.axis_index("chan")
    whitened_own = whiten(spectra)
    lag_basis = make_basis(FREQ, LAGS)
    width = whitened_own.shape[1]
    block_start = (own_index - 1) * (width // CH)
    whitened = with_halo(whitened_own, (("chan", 1),), width)
    local_blocks = pair_blocks - block_start
    all_dest, all_count = (
        lax.all_gather(pair_dest, "chan", axis=0, tiled=True),
        lax.all_gather(pair_count, "chan", axis=0, tiled=True),
    )
    in_use, present, chosen = sending_plan(pair_dest, pair_count, dev_count)
    filled, source = receiving_plan(all_dest, all_count, own_index, slot_count)
    matrix = cross_rows(whitened, local_blocks, in_use).reshape(slot_count, CH * CH, 2 * FREQ)
    outgoing = jnp.take(matrix, chosen, axis=0) * present[:, None, None].astype(jnp.bfloat16)
    placed = jnp.take(
        lax.all_to_all(outgoing, "chan", split_axis=0, concat_axis=0, tiled=True), source, axis=0
    ) * filled[:, None, None].astype(jnp.bfloat16)
    return jnp.dot(placed, lag_basis, preferred_element_type=jnp.float32)


def solution(mesh):
    in_specs = (
        P(None, ("parts", "chan"), None, None),
        P(("parts", "chan"), None),
        P(("parts", "chan"), None),
        P(("parts", "chan")),
    )
    out_specs = P(("parts", "chan"), None, None)
    return jax.shard_map(shards, mesh=mesh, in_specs=in_specs, out_specs=out_specs, check_vma=False)
```

profile of v0, /device:TPU:0, one launch (start us, length us, event | category | flops | bytes accessed | tf_op | source)
XLA Modules:
  0.0 880.8 jit_solution(13032593994910557263)
XLA Ops:
  0.0 1.1 fusion.19
  1.2 1.1 fusion.20
  2.2 2.4 collective-permute-start
  4.6 1.3 collective-permute-start.1
  6.6 0.7 slice_bitcast_fusion
  7.3 0.1 select_reduce_fusion.2
  7.4 0.6 compare_and_fusion.1
  8.0 0.1 fusion.25
  8.1 0.7 broadcast_subtract_fusion
  8.8 1.3 dynamic-slice
  10.1 0.8 dynamic-update-slice
  10.9 16.4 %all-reduce = s32[16]{0:T(128)} all-reduce(s32[16]{0:T(128)S(1)} %dynamic-update-slice), channel_id=1, replica_groups=mesh['parts'=2,'chan'=16] {'chan'}, use_global_device_ids=true, to_apply=%add | all-reduce | flops 16 | bytes 128
  27.4 0.6 convert_element_type.60
  27.9 0.6 pad_clamp_fusion.1
  28.5 0.5 pad_maximum_fusion.5
  29.1 0.3 reshape.132
  29.3 0.5 fusion.14
  29.8 0.8 reshape.133
  30.6 1.6 stack_reshape.3
  32.2 2.2 fusion.35
  34.5 0.6 copy.35
  35.0 0.6 copy_negate_fusion
  35.7 0.1 pad_maximum_fusion.4
  35.8 36.2 %copy.26 = bf16[2,16,4,2,2048]{2,0,3,4,1:T(2,128)(2,1)} copy(bf16[2,16,4,2,2048]{4,1,3,2,0:T(8,128)(2,1)S(1)} %pad_maximum_fusion.4) | data formatting | bytes 2097152 | tf_op jit(solution)/shard_map/stack | solution.py:62
  72.0 58.4 %copy.27 = bf16[2,16,4,1,2,2048]{2,0,4,3,5,1:T(2,128)(2,1)} copy(bf16[2,16,4,1,2,2048]{5,4,2,1,0,3:T(2,128)(2,1)S(1)} %copy-done) | data formatting | bytes 2097152 | tf_op jit(solution)/shard_map/stack;reshape | solution.py:63
  130.4 0.5 fusion.15
  130.9 0.8 reshape.134
  131.7 58.6 %copy.30 = bf16[2,16,4,2,2048,1]{2,0,3,5,4,1:T(2,128)(2,1)} copy(bf16[2,16,4,2,2048,1]{4,3,2,1,0,5:T(2,128)(2,1)S(1)} %bitcast.84) | data formatting | bytes 2097152 | tf_op jit(solution)/shard_map/reshape | solution.py:58
  190.3 110.9 %pad_maximum_fusion.8 = bf16[2,16,4,2,2,2048]{2,0,4,3,5,1:T(2,128)(2,1)} fusion(bf16[2,16,4,1,2,2048]{2,0,4,3,5,1:T(2,128)(2,1)} %bitcast.83, bf16[2,16,4,1,2,2048]{2,0,4,3,5,1:T(2,128)(2,1)} %copy.27), kind=kLoop, calls=%fused_computation.13.clone.clone.clone.clone.1 | loop fusion | flops 1048576 | bytes 4194304 | tf_op jit(solution)/shard_map/sripf,srjcpf->rijcf/dot_general | solution.py:64
  301.3 146.4 %fusion.11 = bf16[16,4,4,2,2048]{1,2,3,4,0:T(4,128)(2,1)} fusion(f32[16]{0:T(128)S(1)} %broadcast_select_fusion, bf16[2,16,4,2,2048,1]{2,0,3,5,4,1:T(2,128)(2,1)} %copy.30, bf16[2,16,4,2,2,2048]{2,0,4,3,5,1:T(2,128)(2,1)} %pad_maximum_fusion.8), kind=kOutput, calls=%fused_computation.19 | convolution fusion | flops 10485760 | bytes 5242944 | tf_op jit(solution)/shard_map/sripf,srjcpf->rijcf/dot_general | solution.py:64
  447.7 96.1 %copy.29 = bf16[16,4,4,2,2048]{4,3,2,1,0:T(2,128)(2,1)S(1)} copy(bf16[16,4,4,2,2048]{1,2,3,4,0:T(4,128)(2,1)} %fusion.11) | data formatting | bytes 4194304 | tf_op jit(solution)/shard_map/convert_element_type | solution.py:69
  543.7 2.8 reshape_reshape.3
  546.5 2.4 gather_fusion
  549.0 1.6 select_multiply_fusion.2
  550.5 4.4 all-to-all-start
  555.0 0.7 fusion.36
  556.0 4.4 compare_select_fusion.1
  560.4 5.6 select_select_fusion
  566.1 39.1 %all-gather = s32[16,16,2]{1,2,0:T(2,128)S(1)} all-gather(s32[1,16,2]{1,2,0:T(2,128)S(1)} %bitcast.88), channel_id=1, replica_groups=mesh['parts'=2,'chan'=16] {'chan'}, dimensions={0}, use_global_device_ids=true | all-gather | bytes 2176 | tf_op jit(solution)/shard_map/all_gather | solution.py:108
  605.1 0.1 reshape.217
  605.3 0.1 eq.100
  605.4 0.1 select_reduce_fusion.1
  605.6 0.1 fusion.23
  605.8 3.8 iota_multiply_fusion
  609.7 251.5 %fusion.6 = bf16[4096,4096]{1,0:T(8,128)(2,1)} fusion(s32[4096]{0:T(1024)S(1)} %bitcast.86, s32[2048,4096]{1,0:T(8,128)S(1)} %iota_multiply_fusion, f32[4096]{0:T(1024)S(1)} %bitcast.85), kind=kLoop, calls=%fused_computation.12 | loop fusion | flops 268435456 | bytes 67141632 | tf_op jit(solution)/shard_map/convert_element_type | solution.py:39
  861.2 0.1 select_reduce_fusion
  861.4 2.3 gather_fusion.1
  863.6 17.2 %fusion.12 = f32[16,16,4096]{2,1,0:T(8,128)} fusion(bf16[4096,4096]{1,0:T(8,128)(2,1)} %fusion.6, bf16[16,16,4096]{2,1,0:T(8,128)(2,1)S(1)} %gather_fusion.1, pred[16]{0:T(512)(128)(4,1)S(1)} %compare_and_fusion, bf16[16]{0:T(256)(128)(2,1)S(1)} %convert_element_type.61), kind=kOutput, calls=%fused_computation.20 | convolution fusion | flops 8592031744 | bytes 39845936 | tf_op jit(solution)/shard_map/dot_general | solution.py:118
  (43 shorter events, 0.7 us)
Async XLA Ops:
  2.2 26.3 %collective-permute-start = (bf16[2,8,2,2048]{3,2,1,0:T(2,128)(2,1)S(1)}, bf16[2,8,2,2048]{3,2,1,0:T(2,128)(2,1)S(1)}, u32[]{:S(2)}, u32[]{:S(2)}) collective-permute-start(bf16[2,8,2,2048]{3,2,1,0:T(2,128)(2,1)S(1)} %fusion.20), channel_id=1, source_target_pairs={{0,1},{1,2},{2,3},{3,4},{4,5},{5,6},{6,7},{7,8},{8,9},{9,10},{10,1... | collective-permute-start | bytes 393224 | tf_op jit(solution)/shard_map/ppermute | solution.py:21
  4.6 23.9 %collective-permute-start.1 = (bf16[2,8,2,2048]{3,2,1,0:T(2,128)(2,1)S(1)}, bf16[2,8,2,2048]{3,2,1,0:T(2,128)(2,1)S(1)}, u32[]{:S(2)}, u32[]{:S(2)}) collective-permute-start(bf16[2,8,2,2048]{3,2,1,0:T(2,128)(2,1)S(1)} %fusion.20), channel_id=1, source_target_pairs={{1,0},{2,1},{3,2},{4,3},{5,4},{6,5},{7,6},{8,7},{9,8},{10,9},{11,1... | collective-permute-start | bytes 393224 | tf_op jit(solution)/shard_map/ppermute | solution.py:23
  32.2 39.8 %copy-start = (bf16[2,16,4,1,2,2048]{5,4,2,1,0,3:T(2,128)(2,1)S(1)}, bf16[2,16,4,1,2,2048]{5,4,2,1,0,3:T(2,128)(2,1)}, u32[]{:S(2)}) copy-start(bf16[2,16,4,1,2,2048]{5,4,2,1,0,3:T(2,128)(2,1)} %stack_reshape.3) | copy-start | bytes 3145732
  447.6 101.3 %copy-start.3 = (pred[16]{0:T(512)(128)(4,1)S(1)}, pred[16]{0:T(512)(128)(4,1)}, u32[]{:S(2)}) copy-start(pred[16]{0:T(512)(128)(4,1)} %compare_and_fusion.1) | copy-start | bytes 52
  447.6 101.3 %copy-start.4 = (bf16[16]{0:T(256)(128)(2,1)S(1)}, bf16[16]{0:T(256)(128)(2,1)}, u32[]{:S(2)}) copy-start(bf16[16]{0:T(256)(128)(2,1)} %convert_element_type.60) | copy-start | bytes 100
  447.7 107.3 %copy-start.1 = (s32[16]{0:T(128)S(1)}, s32[16]{0:T(128)}, u32[]{:S(2)}) copy-start(s32[16]{0:T(128)} %all-reduce) | copy-start | bytes 196
  447.7 118.4 %copy-start.2 = (s32[16,2]{0,1:T(2,128)S(1)}, s32[16,2]{0,1:T(2,128)}, u32[]{:S(2)}) copy-start(s32[16,2]{0,1:T(2,128)} %param.8) | copy-start | bytes 388
  550.5 310.8 %all-to-all-start = ((bf16[16,16,4096]{2,1,0:T(8,128)(2,1)}), bf16[16,16,4096]{2,1,0:T(8,128)(2,1)}, u32[]{:S(2)}, u32[]{:S(2)}) async-start(bf16[16,16,4096]{2,1,0:T(8,128)(2,1)} %select_multiply_fusion.2), calls=%async_computation | async-start | bytes 4194304 | tf_op jit(solution)/shard_map/all_to_all | solution.py:116
where the time goes:
time: 890 us; the launch traced here: 881 us
  other arithmetic  385 us (43%)
  local copies, waits for them, and re-layouts  267 us (30%)
  matrix products  165 us (19%)
  blocking collectives  55.5 us (6%)
    convert_element_type x1, other arithmetic, make_basis(): (weight * jnp.cos(angles)).astype(jnp.bfloat16).reshape(2 * bin_count, lags)  252 us
    dot_general x1, matrix products, cross_rows(): jnp.einsum('sripf,srjcpf->rijcf', first_side, both_sides, preferred_eleme...  146 us
    dot_general x1, other arithmetic, cross_rows(): jnp.einsum('sripf,srjcpf->rijcf', first_side, both_sides, preferred_eleme...  111 us
    convert_element_type x1, local copies, waits for them, and re-layouts, cross_rows(): stacked.astype(jnp.bfloat16)  96.1 us
    reshape x3, local copies, waits for them, and re-layouts, select(): picked.astype(jnp.bfloat16)  60.2 us
    another operation x2, local copies, waits for them, and re-layouts, cross_rows(): both_sides = jnp.stack([second_side, rotated], axis=3)  60 us
    all_gather x1, blocking collectives, shards(): lax.all_gather(pair_dest, 'chan', axis=0, tiled=True)  39.1 us
    another operation x1, local copies, waits for them, and re-layouts, cross_rows(): jnp.stack([-second_side[:, :, :, 1, :], second_side[:, :, :, 0, :]], axis=3)  36.2 us
  transfers between devices with their start and end apart: 3, of which 0 were waited for; matrix products, arithmetic and copies ran while one was open for 31% of the time, Pallas kernels for 0%

commit v1 on v0

v1 whole, which is shorter than its diff:
```python
import functools
import math

import jax
import jax.numpy as jnp
import ml_dtypes
import numpy as np
from jax import lax
from jax.experimental import pallas as pl
from jax.experimental.pallas import tpu as pltpu
from jax.sharding import PartitionSpec as P

LAGS = 4096
FREQ = 2048
CH = 4
RADIX = 16
BINS = FREQ // RADIX
SPAN = LAGS // RADIX
PAIRS = RADIX // 2
MESH = pl.DeviceIdType.MESH


def stage_basis():
    fb = np.arange(BINS)
    nb = np.arange(SPAN)

    def parts(fa):
        f = fa + RADIX * fb
        weight = np.where(f == 0, 1.0, 2.0)[:, None] / (2.0 * math.sqrt(FREQ))
        angle = (f[:, None] * nb[None, :] % LAGS) * (2.0 * math.pi / LAGS)
        c, s = weight * np.cos(angle), weight * np.sin(angle)
        return np.concatenate([c, -s]), np.concatenate([s, c])

    out = np.zeros((PAIRS, 4 * BINS, 2 * SPAN))
    for q in range(PAIRS):
        low = parts(q)
        high = parts(RADIX - q if q else PAIRS)
        if q:
            out[q] = np.block([[low[0], low[1]], [high[0], -high[1]]])
        else:
            zero = np.zeros_like(low[0])
            out[q] = np.block([[low[0], zero], [zero, high[0]]])
    return out.astype(ml_dtypes.bfloat16)


def gather_kernel(n, x_ref, meta_ref, all_ref, piece, own_sem, send_sems, recv_sems):
    me = lax.axis_index("chan")
    nz = n // 4
    z, y, c = me // 4, (me // 2) % 2, me % 2

    def index(zz, yy, cc):
        return (zz * 2 + yy) * 2 + cc

    def far(k):
        out, bit = 0, 1
        while bit < nz:
            out = out + (((z // bit) + (k // bit)) % 2) * bit
            bit *= 2
        return out

    zs = [far(k) for k in range(1, nz)]
    other_y, other_c = index(z, 1 - y, c), index(z, y, 1 - c)
    partners = [index(zz, y, c) for zz in zs] + [other_y, other_c]
    barrier = pltpu.get_barrier_semaphore()
    for dev in partners:
        pl.semaphore_signal(barrier, inc=1, device_id={"chan": dev}, device_id_type=MESH)

    rows = x_ref.shape[0]
    half = rows // 2
    values = x_ref[...].astype(jnp.float32)
    power = jnp.sum(values * values, axis=1, keepdims=True)
    mean_power = (power[:half] + power[half:]) * (1.0 / (2 * FREQ))
    root = jnp.sqrt(mean_power + 1e-06)
    white = (values / jnp.concatenate([root, root], axis=0)).astype(jnp.bfloat16)
    groups = FREQ // 256
    stacked = jnp.concatenate([white[:, g * 256 : (g + 1) * 256] for g in range(groups)], axis=0)
    src = lax.broadcasted_iota(jnp.int32, (256, 256), 0)
    dst = lax.broadcasted_iota(jnp.int32, (256, 256), 1)
    perm = ((src & 15) * 16 + (src >> 4) == dst).astype(jnp.float32).astype(jnp.bfloat16)
    sorted_bins = jnp.dot(stacked, perm, preferred_element_type=jnp.float32)
    place = lax.broadcasted_iota(jnp.int32, (rows, 128), 1) >> 4
    for h in range(2):
        turned = []
        for g in range(groups):
            t = sorted_bins[g * rows : (g + 1) * rows, h * 128 : (h + 1) * 128]
            turned.append(pltpu.roll(t, g * 16, 1) if g else t)
        for fl in range(8):
            t = turned[0]
            for g in range(1, groups):
                t = jnp.where(place == (fl + g) % 8, turned[g], t)
            if fl:
                t = pltpu.roll(t, 128 - fl * 16, 1)
            t = t.astype(jnp.bfloat16)
            piece[h * 8 + fl, :, 0:128] = t[:half]
            piece[h * 8 + fl, :, 128:256] = t[half:]
    piece[RADIX] = meta_ref[...]

    own = pltpu.make_async_copy(piece, all_ref.at[me], own_sem)
    own.start()
    pl.semaphore_wait(barrier, len(partners))
    copies = []

    def send(what, dev, src_ref=None):
        copy = pltpu.make_async_remote_copy(
            src_ref=all_ref.at[what] if src_ref is None else src_ref,
            dst_ref=all_ref.at[what],
            send_sem=send_sems.at[len(copies)],
            recv_sem=recv_sems.at[what],
            device_id={"chan": dev},
            device_id_type=MESH,
        )
        copy.start()
        copies.append(copy)

    def arrived(what):
        pltpu.make_async_remote_copy(
            src_ref=all_ref.at[what],
            dst_ref=all_ref.at[what],
            send_sem=send_sems.at[0],
            recv_sem=recv_sems.at[what],
            device_id={"chan": other_c},
            device_id_type=MESH,
        ).wait_recv()

    send(me, other_y, piece)
    for zz in zs:
        send(me, index(zz, y, c), piece)
    send(me, other_c, piece)
    arrived(other_y)
    send(other_y, other_c)
    for zz in zs:
        what = index(zz, y, c)
        arrived(what)
        send(what, other_y)
        send(what, other_c)
    for zz in zs:
        what = index(zz, 1 - y, c)
        arrived(what)
        send(what, other_c)
    for zz in [z] + zs:
        for yy in (y, 1 - y):
            arrived(index(zz, yy, 1 - c))
    own.wait()
    for copy in copies:
        copy.wait_send()


def gather(n, x, meta):
    rows = x.shape[0] // 2
    shape = (RADIX + 1, rows, 2 * BINS)
    return pl.pallas_call(
        functools.partial(gather_kernel, n),
        out_shape=jax.ShapeDtypeStruct((n,) + shape, jnp.bfloat16),
        in_specs=[pl.BlockSpec(memory_space=pltpu.VMEM)] * 2,
        out_specs=pl.BlockSpec(memory_space=pl.ANY),
        scratch_shapes=[
            pltpu.VMEM(shape, jnp.bfloat16),
            pltpu.SemaphoreType.DMA,
            pltpu.SemaphoreType.DMA((n - 1,)),
            pltpu.SemaphoreType.DMA((n,)),
        ],
        compiler_params=pltpu.CompilerParams(
            collective_id=0, has_side_effects=True, vmem_limit_bytes=16 * 1024 * 1024
        ),
    )(x, meta)


def transform(coef, put):
    cos = [math.cos(2 * math.pi * k / 16) for k in range(16)]
    sin = [math.sin(2 * math.pi * k / 16) for k in range(16)]
    a = [coef(0)] + [coef(2 * q) for q in range(1, 8)]
    b = [None] + [coef(2 * q + 1) for q in range(1, 8)]
    a8 = coef(1)
    s08, d08 = a[0] + a8, a[0] - a8
    ee = [s08 + a[4], d08 - b[4], s08 - a[4], d08 + b[4]]
    sa, da, sb, db = a[2] + a[6], a[2] - a[6], b[2] + b[6], b[2] - b[6]
    r = cos[2]
    eo = [sa, r * (da - sb), -db, -(r * (da + sb))]
    even = [ee[k] + eo[k] for k in range(4)] + [ee[k] - eo[k] for k in range(4)]
    p1, m1, p3, m3 = a[1] + a[7], a[1] - a[7], a[3] + a[5], a[3] - a[5]
    bp1, bm1, bp3, bm3 = b[1] + b[7], b[1] - b[7], b[3] + b[5], b[3] - b[5]
    for k in range(8):
        u1, u3 = (p1, p3) if k % 2 == 0 else (m1, m3)
        v1, v3 = (bm1, bm3) if k % 2 == 0 else (bp1, bp3)
        k3 = 3 * k % 16
        if k == 0:
            odd = u1 + u3
        elif k == 4:
            odd = v3 - v1
        else:
            odd = cos[k] * u1 - sin[k] * v1 + cos[k3] * u3 - sin[k3] * v3
        put(k, even[k] + odd)
        put(k + 8, even[k] - odd)


def stack_kernel(n, slots, chunk, low_ref, high_ref, meta_ref, basis_ref, out_ref, pick, coefs):
    step = pl.program_id(0)
    rows = slots * CH * CH
    depth = n * low_ref.shape[2]

    @pl.when(step == 0)
    def _():
        me = lax.axis_index("chan").astype(jnp.float32)
        slot = lax.broadcasted_iota(jnp.int32, (slots, 2 * BINS), 0).astype(jnp.float32)
        found_a = jnp.zeros((slots, 2 * BINS), jnp.float32)
        found_b = jnp.zeros((slots, 2 * BINS), jnp.float32)
        for d in range(n):
            lists = meta_ref[d, 0].astype(jnp.float32)
            here = jnp.logical_and(lists[0:1] == me, lists[1:2] == slot)
            found_a = jnp.where(here, lists[2:3], found_a)
            found_b = jnp.where(here, lists[3:4], found_b)

        def spread(found):
            total = jnp.sum(found, axis=1, keepdims=True) - 1.0
            wide = jnp.broadcast_to(total, (slots, depth))
            wide = jnp.broadcast_to(wide[:, None, :], (slots, CH * CH, depth))
            return wide.reshape(rows, depth).astype(jnp.int32)

        row = lax.broadcasted_iota(jnp.int32, (rows, depth), 0)
        column = lax.broadcasted_iota(jnp.int32, (rows, depth), 1)
        channel = (column >> 4) * 8 + (column & 7)
        segment = (column >> 3) & 1
        for side, found in enumerate((found_a, found_b)):
            member = (row >> 2) & 3 if side == 0 else row & 3
            same = channel == spread(found) * CH + member
            for s in range(2):
                hit = jnp.where(jnp.logical_and(same, segment == s), 1.0, 0.0)
                k = (side * 2 + s) * rows
                pick[k : k + rows, :] = hit.astype(jnp.bfloat16)

    @pl.when(step < PAIRS)
    def _():
        crosses = []
        for ref in (low_ref, high_ref):
            white = ref[:, 0].reshape(depth, 2 * BINS)
            found = jnp.dot(pick[...], white, preferred_element_type=jnp.float32)
            re, im = 0.0, 0.0
            for s in range(2):
                left = found[s * rows : (s + 1) * rows]
                right = found[(2 + s) * rows : (3 + s) * rows]
                l0, l1 = left[:, :BINS], left[:, BINS:]
                r0, r1 = right[:, :BINS], right[:, BINS:]
                re = re + (l0 * r0 + l1 * r1)
                im = im + (l1 * r0 - l0 * r1)
            crosses += [(re * 0.5).astype(jnp.bfloat16), (im * 0.5).astype(jnp.bfloat16)]
        cross = jnp.concatenate(crosses, axis=1)
        coefs[step] = jnp.dot(cross, basis_ref[0], preferred_element_type=jnp.float32)

    @pl.when(step >= PAIRS)
    def _():
        base = (step - PAIRS) * chunk

        def body(i, carry):
            for h in range(SPAN // 128):
                def coef(k):
                    col = (k % 2) * SPAN + h * 128
                    at = pl.ds(pl.multiple_of(base + i * 8, 8), 8)
                    return coefs[k // 2, at, col : col + 128]

                def put(na, value):
                    col = na * SPAN + h * 128
                    out_ref[pl.ds(pl.multiple_of(i * 8, 8), 8), col : col + 128] = value

                transform(coef, put)
            return carry

        lax.fori_loop(0, chunk // 8, body, 0)


def stack(n, slots, pieces, basis):
    rows = slots * CH * CH
    half = pieces.shape[2]
    chunk = 64
    block = (n, 1, half, 2 * BINS)

    def low(i):
        return (0, jnp.minimum(i, PAIRS - 1), 0, 0)

    def high(i):
        return (0, jnp.where(i == 0, PAIRS, jnp.maximum(RADIX - i, PAIRS + 1)), 0, 0)

    return pl.pallas_call(
        functools.partial(stack_kernel, n, slots, chunk),
        out_shape=jax.ShapeDtypeStruct((rows, LAGS), jnp.float32),
        grid=(PAIRS + rows // chunk,),
        in_specs=[
            pl.BlockSpec(block, low),
            pl.BlockSpec(block, high),
            pl.BlockSpec(block, lambda i: (0, RADIX, 0, 0)),
            pl.BlockSpec((1, 4 * BINS, 2 * SPAN), lambda i: (jnp.minimum(i, PAIRS - 1), 0, 0)),
        ],
        out_specs=pl.BlockSpec((chunk, LAGS), lambda i: (jnp.maximum(i - PAIRS, 0), 0)),
        scratch_shapes=[
            pltpu.VMEM((4 * rows, n * half), jnp.bfloat16),
            pltpu.VMEM((PAIRS, rows, 2 * SPAN), jnp.float32),
        ],
        compiler_params=pltpu.CompilerParams(vmem_limit_bytes=40 * 1024 * 1024),
    )(pieces, pieces, pieces, basis)


def shards(basis, spectra, pair_blocks, pair_dest, pair_count):
    slots = pair_dest.shape[0]
    n = lax.axis_size("chan")
    x = spectra.transpose(2, 0, 1, 3).reshape(-1, FREQ)
    used = jnp.arange(slots, dtype=jnp.int32) < pair_count[0]
    lists = jnp.stack(
        [
            jnp.where(used, pair_dest[:, 0], -1),
            pair_dest[:, 1],
            pair_blocks[:, 0] + 1,
            pair_blocks[:, 1] + 1,
        ]
    )
    half = x.shape[0] // 2
    meta = jnp.pad(
        lists, ((0, half - 4), (0, 2 * BINS - slots)), constant_values=-1
    ).astype(jnp.bfloat16)
    pieces = gather(n, x, meta)
    out = stack(n, slots, pieces, jnp.asarray(basis))
    return out.reshape(slots, CH * CH, LAGS)


def solution(mesh):
    in_specs = (
        P(None, ("parts", "chan"), None, None),
        P(("parts", "chan"), None),
        P(("parts", "chan"), None),
        P(("parts", "chan")),
    )
    out_specs = P(("parts", "chan"), None, None)
    return jax.shard_map(
        functools.partial(shards, stage_basis()),
        mesh=mesh,
        in_specs=in_specs,
        out_specs=out_specs,
        check_vma=False,
    )
```

time: 890 us -> 39.6 us (0.04); the launches traced: 881 us -> 39.4 us
  other arithmetic: 385 us -> 2.14 us
  local copies, waits for them, and re-layouts: 267 us -> 3.14 us
  matrix products: 165 us -> 0 us
  blocking collectives: 55.5 us -> 0 us
  Pallas kernels: 0 us -> 33.5 us
    convert_element_type x4 -> x0, other arithmetic: 253 us -> none  [the longest x1 252 us: make_basis(): (weight * jnp.cos(angles)).astype(jnp.bfloat16).reshape(2 * bin_count, lags)]
    dot_general x4 -> x0, matrix products: 165 us -> none  [the longest x1 146 us: cross_rows(): jnp.einsum('sripf,srjcpf->rijcf', first_side, both_sides, preferred_eleme...]
    dot_general x1 -> x0, other arithmetic: 111 us -> none  [cross_rows(): jnp.einsum('sripf,srjcpf->rijcf', first_side, both_sides, preferred_eleme...]
    another operation x4 -> x1, local copies, waits for them, and re-layouts: 99 us -> 0.01 us  [shards(): jnp.stack([jnp.where(used, pair_dest[:, 0], -1), pair_dest[:, 1], pair_bl...]
    convert_element_type x1 -> x0, local copies, waits for them, and re-layouts: 96.1 us -> none  [cross_rows(): stacked.astype(jnp.bfloat16)]
    reshape x4 -> x0, local copies, waits for them, and re-layouts: 60.5 us -> none  [the longest x3 60.2 us: select(): picked.astype(jnp.bfloat16)]
    all_gather x1 -> x0, blocking collectives: 39.1 us -> none  [shards(): lax.all_gather(pair_dest, 'chan', axis=0, tiled=True)]
    pallas_call x0 -> x2, Pallas kernels: none -> 33.5 us  [the longest x1 24.4 us: gather(): pl.pallas_call(functools.partial(gather_kernel, n), out_shape=jax.ShapeDt...]
  transfers between devices with their start and end apart: 3 -> 0, of which waited for: 0 -> 0; matrix products, arithmetic and copies ran while one was open for 31% -> 0% of each run, Pallas kernels for 0% -> 0%
where the time goes in v1:
time: 39.6 us; the launch traced here: 39.4 us
  Pallas kernels  33.5 us (85%)
  local copies, waits for them, and re-layouts  3.14 us (8%)
  other arithmetic  2.14 us (5%)
  between operations  0.67 us (2%)
    pallas_call x1, Pallas kernels, gather(): pl.pallas_call(functools.partial(gather_kernel, n), out_shape=jax.ShapeDt...  24.4 us
    pallas_call x1, Pallas kernels, stack(): pl.pallas_call(functools.partial(stack_kernel, n, slots, chunk), out_shap...  9.05 us
    unnamed x2, local copies, waits for them, and re-layouts  2.18 us
    another operation x2, other arithmetic  1.37 us
    transpose x1, local copies, waits for them, and re-layouts, shards(): x = spectra.transpose(2, 0, 1, 3).reshape(-1, FREQ)  0.95 us

profile of v1, /device:TPU:0, one launch (start us, length us, event | category | flops | bytes accessed | tf_op | source)
XLA Modules:
  0.0 39.4 jit_solution(16391228348265552447)
XLA Ops:
  0.7 0.7 %fusion.12 = bf16[1,16]{1,0:T(2,128)(2,1)S(1)} fusion(s32[16,2]{0,1:T(2,128)} %param.7, s32[]{:T(128)} %bitcast.12), kind=kLoop, calls=%fused_computation.15 | loop fusion | flops 48 | bytes 100 | tf_op jit(solution)/shard_map/convert.2
  1.3 0.7 %convert.19 = bf16[16,2]{0,1:T(2,128)(2,1)S(1)} convert(s32[16,2]{0,1:T(2,128)} %param.7) | non-fusion elementwise | flops 32 | bytes 192 | tf_op jit(solution)/shard_map/convert.9
  2.0 0.8 %convert_bitcast_fusion.1 = (bf16[1,16]{1,0:T(2,128)(2,1)S(1)}, bf16[1,16]{1,0:T(2,128)(2,1)S(1)}) fusion(s32[16,2]{0,1:T(2,128)} %param.6), kind=kLoop, calls=%fused_computation.17 | loop fusion | flops 64 | bytes 192 | tf_op jit(solution)/shard_map/add | solution.py:310
  2.8 0.9 %copy.6 = bf16[2,2,8,2048]{3,2,1,0:T(8,128)(2,1)S(1)} copy(bf16[2,2,8,2048]{3,0,2,1:T(2,128)(2,1)} %bitcast.14) | data formatting | bytes 262144 | tf_op jit(solution)/shard_map/transpose | solution.py:304
  3.8 24.4 %shard_map.55.low_ref.high_ref.meta_ref = bf16[16,17,16,256]{3,2,1,0:T(8,128)(2,1)S(1)} custom-call(bf16[32,2048]{1,0:T(8,128)(2,1)S(1)} %bitcast.13, bf16[16,256]{1,0:T(8,128)(2,1)S(1)} %fusion.8.meta_ref), custom_call_target="tpu_custom_call" | custom-call | tf_op jit(solution)/shard_map/pallas_call | solution.py:151
  28.2 0.0 copy-start
  28.2 2.2 %copy-done = bf16[8,512,512]{2,1,0:T(8,128)(2,1)S(1)} copy-done((bf16[8,512,512]{2,1,0:T(8,128)(2,1)S(1)}, bf16[8,512,512]{2,1,0:T(8,128)(2,1)}, u32[]{:S(2)}) %copy-start) | copy-done | bytes 4194328
  30.4 9.1 %shard_map.56 = f32[256,4096]{1,0:T(8,128)} custom-call(bf16[16,17,16,256]{3,2,1,0:T(8,128)(2,1)S(1)} %shard_map.55.low_ref.high_ref.meta_ref, bf16[16,17,16,256]{3,2,1,0:T(8,128)(2,1)S(1)} %shard_map.55.low_ref.high_ref.meta_ref, bf16[16,17,16,256]{3,2,1,0:T(8,128)(2,1)S(1)} %shard_map.55.low_ref.high_ref.meta_ref, bf16[8,512,512]{2,1,0:T(8,128)(2,1)S(1)} %copy-done), custom_call_target="tpu_custom_call" | custom-call | tf_op jit(solution)/shard_map/pallas_call | solution.py:282
  (2 shorter events, 0.0 us)
Async XLA Ops:
  28.2 2.2 %copy-start = (bf16[8,512,512]{2,1,0:T(8,128)(2,1)S(1)}, bf16[8,512,512]{2,1,0:T(8,128)(2,1)}, u32[]{:S(2)}) copy-start(bf16[8,512,512]{2,1,0:T(8,128)(2,1)} %constant.8.clone.basis_ref) | copy-start | bytes 12582916

commit v2 on v1

--- a/solution.py
+++ b/solution.py
@@ -43,28 +43,48 @@
     return out.astype(ml_dtypes.bfloat16)
 
 
-def gather_kernel(n, x_ref, meta_ref, all_ref, piece, own_sem, send_sems, recv_sems):
+def tile_of(fa):
+    if fa % PAIRS == 0:
+        return fa // PAIRS
+    return 2 * fa if fa < PAIRS else 2 * (RADIX - fa) + 1
+
+
+def gather_kernel(
+    n, count_ref, x_ref, dest_ref, blocks_ref, all_ref, lists, piece, own_sem, send_sems, recv_sems
+):
     me = lax.axis_index("chan")
     nz = n // 4
     z, y, c = me // 4, (me // 2) % 2, me % 2
+    always, up, down = None, z < nz - 1, z > 0
 
     def index(zz, yy, cc):
         return (zz * 2 + yy) * 2 + cc
 
-    def far(k):
-        out, bit = 0, 1
-        while bit < nz:
-            out = out + (((z // bit) + (k // bit)) % 2) * bit
-            bit *= 2
-        return out
-
-    zs = [far(k) for k in range(1, nz)]
+    def under(condition, body):
+        if condition is None:
+            body()
+        else:
+            pl.when(condition)(body)
+
     other_y, other_c = index(z, 1 - y, c), index(z, y, 1 - c)
-    partners = [index(zz, y, c) for zz in zs] + [other_y, other_c]
+    above, below = index(z + 1, y, c), index(z - 1, y, c)
+    partners = [(always, other_y), (always, other_c), (up, above), (down, below)]
     barrier = pltpu.get_barrier_semaphore()
-    for dev in partners:
-        pl.semaphore_signal(barrier, inc=1, device_id={"chan": dev}, device_id_type=MESH)
-
+    for condition, dev in partners:
+        under(
+            condition,
+            lambda dev=dev: pl.semaphore_signal(
+                barrier, inc=1, device_id={"chan": dev}, device_id_type=MESH
+            ),
+        )
+
+    slots = dest_ref.shape[1]
+    used = lax.broadcasted_iota(jnp.int32, (1, slots), 1) < count_ref[0]
+    lists[...] = jnp.full(lists.shape, -1.0, jnp.float32)
+    lists[0:1, 0:slots] = jnp.where(used, dest_ref[0:1, :], -1).astype(jnp.float32)
+    lists[1:2, 0:slots] = dest_ref[1:2, :].astype(jnp.float32)
+    lists[2:4, 0:slots] = (blocks_ref[...] + 1).astype(jnp.float32)
+    piece[RADIX] = lists[...].astype(jnp.bfloat16)
     rows = x_ref.shape[0]
     half = rows // 2
     values = x_ref[...].astype(jnp.float32)
@@ -91,78 +111,101 @@
             if fl:
                 t = pltpu.roll(t, 128 - fl * 16, 1)
             t = t.astype(jnp.bfloat16)
-            piece[h * 8 + fl, :, 0:128] = t[:half]
-            piece[h * 8 + fl, :, 128:256] = t[half:]
-    piece[RADIX] = meta_ref[...]
+            piece[tile_of(h * 8 + fl), :, 0:128] = t[:half]
+            piece[tile_of(h * 8 + fl), :, 128:256] = t[half:]
 
     own = pltpu.make_async_copy(piece, all_ref.at[me], own_sem)
     own.start()
-    pl.semaphore_wait(barrier, len(partners))
+    pl.semaphore_wait(barrier, 2 + (z + nz - 1) // nz + (2 * nz - 2 - z) // nz)
+    halves = [pl.ds(PAIRS, PAIRS + 1), pl.ds(0, PAIRS)]
     copies = []
 
-    def send(what, dev, src_ref=None):
+    def both(first, second):
+        if first is None or second is None:
+            return second if first is None else first
+        return jnp.logical_and(first, second)
+
+    def send(condition, k, what, dev, src_ref=None):
         copy = pltpu.make_async_remote_copy(
-            src_ref=all_ref.at[what] if src_ref is None else src_ref,
-            dst_ref=all_ref.at[what],
+            src_ref=(all_ref.at[what] if src_ref is None else src_ref).at[halves[k]],
+            dst_ref=all_ref.at[what, halves[k]],
             send_sem=send_sems.at[len(copies)],
-            recv_sem=recv_sems.at[what],
+            recv_sem=recv_sems.at[k, what],
             device_id={"chan": dev},
             device_id_type=MESH,
         )
-        copy.start()
-        copies.append(copy)
-
-    def arrived(what):
-        pltpu.make_async_remote_copy(
-            src_ref=all_ref.at[what],
-            dst_ref=all_ref.at[what],
-            send_sem=send_sems.at[0],
-            recv_sem=recv_sems.at[what],
-            device_id={"chan": other_c},
-            device_id_type=MESH,
-        ).wait_recv()
-
-    send(me, other_y, piece)
-    for zz in zs:
-        send(me, index(zz, y, c), piece)
-    send(me, other_c, piece)
-    arrived(other_y)
-    send(other_y, other_c)
-    for zz in zs:
-        what = index(zz, y, c)
-        arrived(what)
-        send(what, other_y)
-        send(what, other_c)
-    for zz in zs:
-        what = index(zz, 1 - y, c)
-        arrived(what)
-        send(what, other_c)
-    for zz in [z] + zs:
-        for yy in (y, 1 - y):
-            arrived(index(zz, yy, 1 - c))
+        copies.append((condition, copy))
+        under(condition, copy.start)
+
+    def arrived(condition, k, what):
+        under(
+            condition,
+            pltpu.make_async_remote_copy(
+                src_ref=all_ref.at[what, halves[k]],
+                dst_ref=all_ref.at[what, halves[k]],
+                send_sem=send_sems.at[0],
+                recv_sem=recv_sems.at[k, what],
+                device_id={"chan": other_c},
+                device_id_type=MESH,
+            ).wait_recv,
+        )
+
+    for k in range(2):
+        send(always, k, me, other_y, piece)
+        send(up, k, me, above, piece)
+        send(down, k, me, below, piece)
+        send(always, k, me, other_c, piece)
+    for t in range(1, nz + 1):
+        for k in range(2):
+            for onward, there, zz, dev in (
+                (up, z >= t, z - t, above),
+                (down, z < nz - t, z + t, below),
+            ):
+                if t < nz:
+                    what = index(zz, y, c)
+                    arrived(there, k, what)
+                    send(there, k, what, other_y)
+                    if t < nz - 1:
+                        send(both(there, onward), k, what, dev)
+                    send(there, k, what, other_c)
+        for k in range(2):
+            if t == 1:
+                arrived(always, k, other_y)
+                send(always, k, other_y, other_c)
+            else:
+                for there, zz in ((z >= t - 1, z - t + 1), (z < nz - t + 1, z + t - 1)):
+                    what = index(zz, 1 - y, c)
+                    arrived(there, k, what)
+                    send(there, k, what, other_c)
+    for k in range(2):
+        for zz in range(nz):
+            for yy in range(2):
+                arrived(always, k, index(zz, yy, 1 - c))
     own.wait()
-    for copy in copies:
-        copy.wait_send()
-
-
-def gather(n, x, meta):
-    rows = x.shape[0] // 2
-    shape = (RADIX + 1, rows, 2 * BINS)
+    for condition, copy in copies:
+        under(condition, copy.wait_send)
+
+
+def gather(n, count, x, dest, blocks):
+    half = x.shape[0] // 2
+    shape = (RADIX + 1, half, 2 * BINS)
+    vmem = pl.BlockSpec(memory_space=pltpu.VMEM)
     return pl.pallas_call(
         functools.partial(gather_kernel, n),
         out_shape=jax.ShapeDtypeStruct((n,) + shape, jnp.bfloat16),
-        in_specs=[pl.BlockSpec(memory_space=pltpu.VMEM)] * 2,
+        in_specs=[pl.BlockSpec(memory_space=pltpu.SMEM), vmem, vmem, vmem],
         out_specs=pl.BlockSpec(memory_space=pl.ANY),
         scratch_shapes=[
+            pltpu.VMEM(shape[1:], jnp.float32),
             pltpu.VMEM(shape, jnp.bfloat16),
             pltpu.SemaphoreType.DMA,
-            pltpu.SemaphoreType.DMA((n - 1,)),
-            pltpu.SemaphoreType.DMA((n,)),
+            pltpu.SemaphoreType.DMA((6 * n,)),
+            pltpu.SemaphoreType.DMA((2, n)),
         ],
         compiler_params=pltpu.CompilerParams(
             collective_id=0, has_side_effects=True, vmem_limit_bytes=16 * 1024 * 1024
         ),
-    )(x, meta)
+    )(count, x, dest, blocks)
 
 
 def transform(coef, put):
@@ -193,19 +236,24 @@
         put(k + 8, even[k] - odd)
 
 
-def stack_kernel(n, slots, chunk, low_ref, high_ref, meta_ref, basis_ref, out_ref, pick, coefs):
+def stack_kernel(n, slots, chunk, all_ref, basis_ref, out_ref, pick, coefs, basis, basis_sems):
     step = pl.program_id(0)
     rows = slots * CH * CH
-    depth = n * low_ref.shape[2]
+    depth = n * all_ref.shape[2]
+
+    def fetch(q):
+        return pltpu.make_async_copy(basis_ref.at[q], basis.at[q], basis_sems.at[q])
 
     @pl.when(step == 0)
     def _():
+        for q in range(PAIRS):
+            fetch(q).start()
         me = lax.axis_index("chan").astype(jnp.float32)
         slot = lax.broadcasted_iota(jnp.int32, (slots, 2 * BINS), 0).astype(jnp.float32)
         found_a = jnp.zeros((slots, 2 * BINS), jnp.float32)
         found_b = jnp.zeros((slots, 2 * BINS), jnp.float32)
         for d in range(n):
-            lists = meta_ref[d, 0].astype(jnp.float32)
+            lists = all_ref[d, RADIX].astype(jnp.float32)
             here = jnp.logical_and(lists[0:1] == me, lists[1:2] == slot)
             found_a = jnp.where(here, lists[2:3], found_a)
             found_b = jnp.where(here, lists[3:4], found_b)
@@ -231,8 +279,8 @@
     @pl.when(step < PAIRS)
     def _():
         crosses = []
-        for ref in (low_ref, high_ref):
-            white = ref[:, 0].reshape(depth, 2 * BINS)
+        for k in range(2):
+            white = all_ref[:, step * 2 + k].reshape(depth, 2 * BINS)
             found = jnp.dot(pick[...], white, preferred_element_type=jnp.float32)
             re, im = 0.0, 0.0
             for s in range(2):
@@ -244,7 +292,8 @@
                 im = im + (l1 * r0 - l0 * r1)
             crosses += [(re * 0.5).astype(jnp.bfloat16), (im * 0.5).astype(jnp.bfloat16)]
         cross = jnp.concatenate(crosses, axis=1)
-        coefs[step] = jnp.dot(cross, basis_ref[0], preferred_element_type=jnp.float32)
+        fetch(step).wait()
+        coefs[step] = jnp.dot(cross, basis[step], preferred_element_type=jnp.float32)
 
     @pl.when(step >= PAIRS)
     def _():
@@ -271,51 +320,30 @@
     rows = slots * CH * CH
     half = pieces.shape[2]
     chunk = 64
-    block = (n, 1, half, 2 * BINS)
-
-    def low(i):
-        return (0, jnp.minimum(i, PAIRS - 1), 0, 0)
-
-    def high(i):
-        return (0, jnp.where(i == 0, PAIRS, jnp.maximum(RADIX - i, PAIRS + 1)), 0, 0)
-
     return pl.pallas_call(
         functools.partial(stack_kernel, n, slots, chunk),
         out_shape=jax.ShapeDtypeStruct((rows, LAGS), jnp.float32),
         grid=(PAIRS + rows // chunk,),
         in_specs=[
-            pl.BlockSpec(block, low),
-            pl.BlockSpec(block, high),
-            pl.BlockSpec(block, lambda i: (0, RADIX, 0, 0)),
-            pl.BlockSpec((1, 4 * BINS, 2 * SPAN), lambda i: (jnp.minimum(i, PAIRS - 1), 0, 0)),
+            pl.BlockSpec(memory_space=pltpu.VMEM),
+            pl.BlockSpec(memory_space=pltpu.HBM),
         ],
         out_specs=pl.BlockSpec((chunk, LAGS), lambda i: (jnp.maximum(i - PAIRS, 0), 0)),
         scratch_shapes=[
             pltpu.VMEM((4 * rows, n * half), jnp.bfloat16),
             pltpu.VMEM((PAIRS, rows, 2 * SPAN), jnp.float32),
+            pltpu.VMEM(basis.shape, jnp.bfloat16),
+            pltpu.SemaphoreType.DMA((PAIRS,)),
         ],
         compiler_params=pltpu.CompilerParams(vmem_limit_bytes=40 * 1024 * 1024),
-    )(pieces, pieces, pieces, basis)
+    )(pieces, basis)
 
 
 def shards(basis, spectra, pair_blocks, pair_dest, pair_count):
     slots = pair_dest.shape[0]
     n = lax.axis_size("chan")
     x = spectra.transpose(2, 0, 1, 3).reshape(-1, FREQ)
-    used = jnp.arange(slots, dtype=jnp.int32) < pair_count[0]
-    lists = jnp.stack(
-        [
-            jnp.where(used, pair_dest[:, 0], -1),
-            pair_dest[:, 1],
-            pair_blocks[:, 0] + 1,
-            pair_blocks[:, 1] + 1,
-        ]
-    )
-    half = x.shape[0] // 2
-    meta = jnp.pad(
-        lists, ((0, half - 4), (0, 2 * BINS - slots)), constant_values=-1
-    ).astype(jnp.bfloat16)
-    pieces = gather(n, x, meta)
+    pieces = gather(n, pair_count, x, pair_dest.T, pair_blocks.T)
     out = stack(n, slots, pieces, jnp.asarray(basis))
     return out.reshape(slots, CH * CH, LAGS)
 

time: 39.6 us -> 36.6 us (0.924)
  Pallas kernels: 33.5 us -> 31.2 us
  other arithmetic: 2.14 us -> 0 us
  local copies, waits for them, and re-layouts: 3.14 us -> 4.48 us
    pallas_call x1, Pallas kernels: 24.4 us -> 21.4 us  [gather(): pl.pallas_call(functools.partial(gather_kernel, n), out_shape=jax.ShapeDt...]
    another operation x3 -> x0, other arithmetic: 1.38 us -> none
    unnamed x2 -> x6, local copies, waits for them, and re-layouts: 2.18 us -> 3.54 us
    add x1 -> x0, other arithmetic: 0.76 us -> none  [shards(): pair_blocks[:, 0] + 1]
    pallas_call x1, Pallas kernels: 9.05 us -> 9.77 us  [stack(): pl.pallas_call(functools.partial(stack_kernel, n, slots, chunk), out_shap...]
where the time goes in v2:
time: 36.6 us; the launch traced here: 36.4 us
  Pallas kernels  31.2 us (85%)
  local copies, waits for them, and re-layouts  4.48 us (12%)
  between operations  0.68 us (2%)
    pallas_call x1, Pallas kernels, gather(): pl.pallas_call(functools.partial(gather_kernel, n), out_shape=jax.ShapeDt...  21.4 us
    pallas_call x1, Pallas kernels, stack(): pl.pallas_call(functools.partial(stack_kernel, n, slots, chunk), out_shap...  9.77 us
    unnamed x6, local copies, waits for them, and re-layouts  3.54 us
    transpose x1, local copies, waits for them, and re-layouts, shards(): x = spectra.transpose(2, 0, 1, 3).reshape(-1, FREQ)  0.95 us

profile of v2, /device:TPU:0, one launch (start us, length us, event | category | flops | bytes accessed | tf_op | source)
XLA Modules:
  0.0 36.4 jit_solution(11259162376516329666)
XLA Ops:
  0.7 0.9 %copy.6 = bf16[2,2,8,2048]{3,2,1,0:T(8,128)(2,1)S(1)} copy(bf16[2,2,8,2048]{3,0,2,1:T(2,128)(2,1)} %bitcast.8) | data formatting | bytes 262144 | tf_op jit(solution)/shard_map/transpose | solution.py:345
  1.6 0.0 copy-start.1
  1.6 0.7 %copy-done.1 = s32[16,2]{0,1:T(2,128)S(1)} copy-done((s32[16,2]{0,1:T(2,128)S(1)}, s32[16,2]{0,1:T(2,128)}, u32[]{:S(2)}) %copy-start.1) | copy-done | bytes 152
  2.3 0.0 copy-start.2
  2.3 0.7 %copy-done.2 = s32[16,2]{0,1:T(2,128)S(1)} copy-done((s32[16,2]{0,1:T(2,128)S(1)}, s32[16,2]{0,1:T(2,128)}, u32[]{:S(2)}) %copy-start.2) | copy-done | bytes 152
  3.0 21.4 %shard_map.55.all_ref = bf16[16,17,16,256]{3,2,1,0:T(8,128)(2,1)S(1)} custom-call(s32[1]{0:T(128)S(6)} %copy.7.count_ref, bf16[32,2048]{1,0:T(8,128)(2,1)S(1)} %bitcast.5, s32[2,16]{1,0:T(2,128)S(1)} %bitcast.6, s32[2,16]{1,0:T(2,128)S(1)} %bitcast.7), custom_call_target="tpu_custom_call" | custom-call | tf_op jit(solution)/shard_map/pallas_call | solution.py:193
  24.4 0.0 copy-start
  24.4 2.2 %copy-done = bf16[8,512,512]{2,1,0:T(8,128)(2,1)S(1)} copy-done((bf16[8,512,512]{2,1,0:T(8,128)(2,1)S(1)}, bf16[8,512,512]{2,1,0:T(8,128)(2,1)}, u32[]{:S(2)}) %copy-start) | copy-done | bytes 4194328
  26.6 9.8 %shard_map.56 = f32[256,4096]{1,0:T(8,128)} custom-call(bf16[16,17,16,256]{3,2,1,0:T(8,128)(2,1)S(1)} %shard_map.55.all_ref, bf16[8,512,512]{2,1,0:T(8,128)(2,1)S(1)} %copy-done), custom_call_target="tpu_custom_call" | custom-call | tf_op jit(solution)/shard_map/pallas_call | solution.py:323
Async XLA Ops:
  1.6 0.7 %copy-start.1 = (s32[16,2]{0,1:T(2,128)S(1)}, s32[16,2]{0,1:T(2,128)}, u32[]{:S(2)}) copy-start(s32[16,2]{0,1:T(2,128)} %param.7) | copy-start | bytes 388
  2.3 0.7 %copy-start.2 = (s32[16,2]{0,1:T(2,128)S(1)}, s32[16,2]{0,1:T(2,128)}, u32[]{:S(2)}) copy-start(s32[16,2]{0,1:T(2,128)} %param.6) | copy-start | bytes 388
  24.4 2.2 %copy-start = (bf16[8,512,512]{2,1,0:T(8,128)(2,1)S(1)}, bf16[8,512,512]{2,1,0:T(8,128)(2,1)}, u32[]{:S(2)}) copy-start(bf16[8,512,512]{2,1,0:T(8,128)(2,1)} %constant.2.clone.basis_ref) | copy-start | bytes 12582916

commit v3 on v2

--- a/solution.py
+++ b/solution.py
@@ -49,8 +49,74 @@
     return 2 * fa if fa < PAIRS else 2 * (RADIX - fa) + 1
 
 
+def fill_pick(n, slots, all_ref, pick):
+    rows = slots * CH * CH
+    depth = n * all_ref.shape[2]
+    me = lax.axis_index("chan").astype(jnp.float32)
+    slot = lax.broadcasted_iota(jnp.int32, (slots, 2 * BINS), 0).astype(jnp.float32)
+    found_a = jnp.zeros((slots, 2 * BINS), jnp.float32)
+    found_b = jnp.zeros((slots, 2 * BINS), jnp.float32)
+    for d in range(n):
+        lists = all_ref[d, RADIX].astype(jnp.float32)
+        here = jnp.logical_and(lists[0:1] == me, lists[1:2] == slot)
+        found_a = jnp.where(here, lists[2:3], found_a)
+        found_b = jnp.where(here, lists[3:4], found_b)
+
+    def spread(found):
+        total = jnp.sum(found, axis=1, keepdims=True) - 1.0
+        wide = jnp.broadcast_to(total, (slots, depth))
+        wide = jnp.broadcast_to(wide[:, None, :], (slots, CH * CH, depth))
+        return wide.reshape(rows, depth).astype(jnp.int32)
+
+    row = lax.broadcasted_iota(jnp.int32, (rows, depth), 0)
+    column = lax.broadcasted_iota(jnp.int32, (rows, depth), 1)
+    channel = (column >> 4) * 8 + (column & 7)
+    segment = (column >> 3) & 1
+    for side, found in enumerate((found_a, found_b)):
+        member = (row >> 2) & 3 if side == 0 else row & 3
+        same = channel == spread(found) * CH + member
+        for s in range(2):
+            hit = jnp.where(jnp.logical_and(same, segment == s), 1.0, 0.0)
+            k = (side * 2 + s) * rows
+            pick[k : k + rows, :] = hit.astype(jnp.bfloat16)
+
+
+def cross_step(rows, q, all_ref, pick, basis, coef_ref):
+    depth = all_ref.shape[0] * all_ref.shape[2]
+    crosses = []
+    for k in range(2):
+        white = all_ref[:, q * 2 + k].reshape(depth, 2 * BINS)
+        found = jnp.dot(pick[...], white, preferred_element_type=jnp.float32)
+        re, im = 0.0, 0.0
+        for s in range(2):
+            left = found[s * rows : (s + 1) * rows]
+            right = found[(2 + s) * rows : (3 + s) * rows]
+            l0, l1 = left[:, :BINS], left[:, BINS:]
+            r0, r1 = right[:, :BINS], right[:, BINS:]
+            re = re + (l0 * r0 + l1 * r1)
+            im = im + (l1 * r0 - l0 * r1)
+        crosses += [(re * 0.5).astype(jnp.bfloat16), (im * 0.5).astype(jnp.bfloat16)]
+    cross = jnp.concatenate(crosses, axis=1)
+    coef_ref[q] = jnp.dot(cross, basis[q], preferred_element_type=jnp.float32)
+
+
 def gather_kernel(
-    n, count_ref, x_ref, dest_ref, blocks_ref, all_ref, lists, piece, own_sem, send_sems, recv_sems
+    n,
+    count_ref,
+    x_ref,
+    dest_ref,
+    blocks_ref,
+    basis_ref,
+    coef_ref,
+    all_ref,
+    lists,
+    piece,
+    pick,
+    basis,
+    own_sem,
+    basis_sems,
+    send_sems,
+    recv_sems,
 ):
     me = lax.axis_index("chan")
     nz = n // 4
@@ -77,6 +143,15 @@
                 barrier, inc=1, device_id={"chan": dev}, device_id_type=MESH
             ),
         )
+
+    fetches = [
+        pltpu.make_async_copy(
+            basis_ref.at[pl.ds(4 * k, 4)], basis.at[pl.ds(4 * k, 4)], basis_sems.at[k]
+        )
+        for k in range(2)
+    ]
+    for fetch in fetches:
+        fetch.start()
 
     slots = dest_ref.shape[1]
     used = lax.broadcasted_iota(jnp.int32, (1, slots), 1) < count_ref[0]
@@ -155,57 +230,96 @@
         send(up, k, me, above, piece)
         send(down, k, me, below, piece)
         send(always, k, me, other_c, piece)
-    for t in range(1, nz + 1):
-        for k in range(2):
-            for onward, there, zz, dev in (
-                (up, z >= t, z - t, above),
-                (down, z < nz - t, z + t, below),
-            ):
-                if t < nz:
-                    what = index(zz, y, c)
-                    arrived(there, k, what)
-                    send(there, k, what, other_y)
-                    if t < nz - 1:
-                        send(both(there, onward), k, what, dev)
-                    send(there, k, what, other_c)
-        for k in range(2):
-            if t == 1:
-                arrived(always, k, other_y)
-                send(always, k, other_y, other_c)
-            else:
-                for there, zz in ((z >= t - 1, z - t + 1), (z < nz - t + 1, z + t - 1)):
-                    what = index(zz, 1 - y, c)
-                    arrived(there, k, what)
-                    send(there, k, what, other_c)
-    for k in range(2):
+
+    def z_step(t, k):
+        for onward, there, zz, dev in (
+            (up, z >= t, z - t, above),
+            (down, z < nz - t, z + t, below),
+        ):
+            what = index(zz, y, c)
+            arrived(there, k, what)
+            send(there, k, what, other_y)
+            if t < nz - 1:
+                send(both(there, onward), k, what, dev)
+            send(there, k, what, other_c)
+
+    def y_step(t, k):
+        if t == 1:
+            arrived(always, k, other_y)
+            send(always, k, other_y, other_c)
+        else:
+            for there, zz in ((z >= t - 1, z - t + 1), (z < nz - t + 1, z + t - 1)):
+                what = index(zz, 1 - y, c)
+                arrived(there, k, what)
+                send(there, k, what, other_c)
+
+    def c_wait(k):
         for zz in range(nz):
             for yy in range(2):
                 arrived(always, k, index(zz, yy, 1 - c))
+
+    rows = slots * CH * CH
+
+    def cross_steps(low, high):
+        def body(q, carry):
+            cross_step(rows, q, all_ref, pick, basis, coef_ref)
+            return carry
+
+        lax.fori_loop(low, high, body, 0)
+
+    for t in range(1, nz):
+        z_step(t, 0)
+        y_step(t, 0)
+        if t > 1:
+            z_step(t - 1, 1)
+            y_step(t - 1, 1)
+    y_step(nz, 0)
+    z_step(nz - 1, 1)
     own.wait()
+    for fetch in fetches:
+        fetch.wait()
+    c_wait(0)
+    fill_pick(n, slots, all_ref, pick)
+    cross_steps(6, 8)
+    y_step(nz - 1, 1)
+    y_step(nz, 1)
+    cross_steps(4, 6)
+    c_wait(1)
+    cross_steps(0, 4)
     for condition, copy in copies:
         under(condition, copy.wait_send)
 
 
-def gather(n, count, x, dest, blocks):
+def limit(rows):
+    return 60 * 1024 * 1024 - rows * LAGS * 8
+
+
+def gather(n, count, x, dest, blocks, basis):
     half = x.shape[0] // 2
+    rows = dest.shape[1] * CH * CH
     shape = (RADIX + 1, half, 2 * BINS)
     vmem = pl.BlockSpec(memory_space=pltpu.VMEM)
+    hbm = pl.BlockSpec(memory_space=pltpu.HBM)
     return pl.pallas_call(
         functools.partial(gather_kernel, n),
-        out_shape=jax.ShapeDtypeStruct((n,) + shape, jnp.bfloat16),
-        in_specs=[pl.BlockSpec(memory_space=pltpu.SMEM), vmem, vmem, vmem],
-        out_specs=pl.BlockSpec(memory_space=pl.ANY),
+        out_shape=jax.ShapeDtypeStruct((PAIRS, rows, 2 * SPAN), jnp.float32),
+        in_specs=[pl.BlockSpec(memory_space=pltpu.SMEM), vmem, vmem, vmem, hbm],
+        out_specs=vmem,
         scratch_shapes=[
+            pltpu.VMEM((n,) + shape, jnp.bfloat16),
             pltpu.VMEM(shape[1:], jnp.float32),
             pltpu.VMEM(shape, jnp.bfloat16),
+            pltpu.VMEM((4 * rows, n * half), jnp.bfloat16),
+            pltpu.VMEM(basis.shape, jnp.bfloat16),
             pltpu.SemaphoreType.DMA,
+            pltpu.SemaphoreType.DMA((2,)),
             pltpu.SemaphoreType.DMA((6 * n,)),
             pltpu.SemaphoreType.DMA((2, n)),
         ],
         compiler_params=pltpu.CompilerParams(
-            collective_id=0, has_side_effects=True, vmem_limit_bytes=16 * 1024 * 1024
+            collective_id=0, has_side_effects=True, vmem_limit_bytes=limit(rows)
         ),
-    )(count, x, dest, blocks)
+    )(count, x, dest, blocks, basis)
 
 
 def transform(coef, put):
@@ -236,115 +350,45 @@
         put(k + 8, even[k] - odd)
 
 
-def stack_kernel(n, slots, chunk, all_ref, basis_ref, out_ref, pick, coefs, basis, basis_sems):
-    step = pl.program_id(0)
-    rows = slots * CH * CH
-    depth = n * all_ref.shape[2]
-
-    def fetch(q):
-        return pltpu.make_async_copy(basis_ref.at[q], basis.at[q], basis_sems.at[q])
-
-    @pl.when(step == 0)
-    def _():
-        for q in range(PAIRS):
-            fetch(q).start()
-        me = lax.axis_index("chan").astype(jnp.float32)
-        slot = lax.broadcasted_iota(jnp.int32, (slots, 2 * BINS), 0).astype(jnp.float32)
-        found_a = jnp.zeros((slots, 2 * BINS), jnp.float32)
-        found_b = jnp.zeros((slots, 2 * BINS), jnp.float32)
-        for d in range(n):
-            lists = all_ref[d, RADIX].astype(jnp.float32)
-            here = jnp.logical_and(lists[0:1] == me, lists[1:2] == slot)
-            found_a = jnp.where(here, lists[2:3], found_a)
-            found_b = jnp.where(here, lists[3:4], found_b)
-
-        def spread(found):
-            total = jnp.sum(found, axis=1, keepdims=True) - 1.0
-            wide = jnp.broadcast_to(total, (slots, depth))
-            wide = jnp.broadcast_to(wide[:, None, :], (slots, CH * CH, depth))
-            return wide.reshape(rows, depth).astype(jnp.int32)
-
-        row = lax.broadcasted_iota(jnp.int32, (rows, depth), 0)
-        column = lax.broadcasted_iota(jnp.int32, (rows, depth), 1)
-        channel = (column >> 4) * 8 + (column & 7)
-        segment = (column >> 3) & 1
-        for side, found in enumerate((found_a, found_b)):
-            member = (row >> 2) & 3 if side == 0 else row & 3
-            same = channel == spread(found) * CH + member
-            for s in range(2):
-                hit = jnp.where(jnp.logical_and(same, segment == s), 1.0, 0.0)
-                k = (side * 2 + s) * rows
-                pick[k : k + rows, :] = hit.astype(jnp.bfloat16)
-
-    @pl.when(step < PAIRS)
-    def _():
-        crosses = []
-        for k in range(2):
-            white = all_ref[:, step * 2 + k].reshape(depth, 2 * BINS)
-            found = jnp.dot(pick[...], white, preferred_element_type=jnp.float32)
-            re, im = 0.0, 0.0
-            for s in range(2):
-                left = found[s * rows : (s + 1) * rows]
-                right = found[(2 + s) * rows : (3 + s) * rows]
-                l0, l1 = left[:, :BINS], left[:, BINS:]
-                r0, r1 = right[:, :BINS], right[:, BINS:]
-                re = re + (l0 * r0 + l1 * r1)
-                im = im + (l1 * r0 - l0 * r1)
-            crosses += [(re * 0.5).astype(jnp.bfloat16), (im * 0.5).astype(jnp.bfloat16)]
-        cross = jnp.concatenate(crosses, axis=1)
-        fetch(step).wait()
-        coefs[step] = jnp.dot(cross, basis[step], preferred_element_type=jnp.float32)
-
-    @pl.when(step >= PAIRS)
-    def _():
-        base = (step - PAIRS) * chunk
-
-        def body(i, carry):
-            for h in range(SPAN // 128):
-                def coef(k):
-                    col = (k % 2) * SPAN + h * 128
-                    at = pl.ds(pl.multiple_of(base + i * 8, 8), 8)
-                    return coefs[k // 2, at, col : col + 128]
-
-                def put(na, value):
-                    col = na * SPAN + h * 128
-                    out_ref[pl.ds(pl.multiple_of(i * 8, 8), 8), col : col + 128] = value
-
-                transform(coef, put)
-            return carry
-
-        lax.fori_loop(0, chunk // 8, body, 0)
-
-
-def stack(n, slots, pieces, basis):
-    rows = slots * CH * CH
-    half = pieces.shape[2]
-    chunk = 64
+def stack_kernel(chunk, coefs, out_ref):
+    base = pl.program_id(0) * chunk
+
+    def body(i, carry):
+        for h in range(SPAN // 128):
+            def coef(k):
+                col = (k % 2) * SPAN + h * 128
+                at = pl.ds(pl.multiple_of(base + i * 8, 8), 8)
+                return coefs[k // 2, at, col : col + 128]
+
+            def put(na, value):
+                col = na * SPAN + h * 128
+                out_ref[pl.ds(pl.multiple_of(i * 8, 8), 8), col : col + 128] = value
+
+            transform(coef, put)
+        return carry
+
+    lax.fori_loop(0, chunk // 8, body, 0)
+
+
+def stack(coefs):
+    rows = coefs.shape[1]
+    chunk = 32
     return pl.pallas_call(
-        functools.partial(stack_kernel, n, slots, chunk),
+        functools.partial(stack_kernel, chunk),
         out_shape=jax.ShapeDtypeStruct((rows, LAGS), jnp.float32),
-        grid=(PAIRS + rows // chunk,),
-        in_specs=[
-            pl.BlockSpec(memory_space=pltpu.VMEM),
-            pl.BlockSpec(memory_space=pltpu.HBM),
-        ],
-        out_specs=pl.BlockSpec((chunk, LAGS), lambda i: (jnp.maximum(i - PAIRS, 0), 0)),
-        scratch_shapes=[
-            pltpu.VMEM((4 * rows, n * half), jnp.bfloat16),
-            pltpu.VMEM((PAIRS, rows, 2 * SPAN), jnp.float32),
-            pltpu.VMEM(basis.shape, jnp.bfloat16),
-            pltpu.SemaphoreType.DMA((PAIRS,)),
-        ],
-        compiler_params=pltpu.CompilerParams(vmem_limit_bytes=40 * 1024 * 1024),
-    )(pieces, basis)
+        grid=(rows // chunk,),
+        in_specs=[pl.BlockSpec(memory_space=pltpu.VMEM)],
+        out_specs=pl.BlockSpec((chunk, LAGS), lambda i: (i, 0)),
+        compiler_params=pltpu.CompilerParams(vmem_limit_bytes=16 * 1024 * 1024),
+    )(coefs)
 
 
 def shards(basis, spectra, pair_blocks, pair_dest, pair_count):
     slots = pair_dest.shape[0]
     n = lax.axis_size("chan")
     x = spectra.transpose(2, 0, 1, 3).reshape(-1, FREQ)
-    pieces = gather(n, pair_count, x, pair_dest.T, pair_blocks.T)
-    out = stack(n, slots, pieces, jnp.asarray(basis))
+    coefs = gather(n, pair_count, x, pair_dest.T, pair_blocks.T, jnp.asarray(basis))
+    out = stack(coefs)
     return out.reshape(slots, CH * CH, LAGS)
 
 

time: 36.6 us -> 39.2 us (1.071)
  Pallas kernels: 31.2 us -> 33.8 us
    pallas_call x1, Pallas kernels: 21.4 us -> 30 us  [gather(): pl.pallas_call(functools.partial(gather_kernel, n), out_shape=jax.ShapeDt...]
    pallas_call x1, Pallas kernels: 9.77 us -> 3.81 us  [stack(): pl.pallas_call(functools.partial(stack_kernel, chunk), out_shape=jax.Shap...]
where the time goes in v3:
time: 39.2 us; the launch traced here: 39 us
  Pallas kernels  33.8 us (86%)
  local copies, waits for them, and re-layouts  4.48 us (11%)
  between operations  0.68 us (2%)
    pallas_call x1, Pallas kernels, gather(): pl.pallas_call(functools.partial(gather_kernel, n), out_shape=jax.ShapeDt...  30 us
    pallas_call x1, Pallas kernels, stack(): pl.pallas_call(functools.partial(stack_kernel, chunk), out_shape=jax.Shap...  3.81 us
    unnamed x6, local copies, waits for them, and re-layouts  3.53 us
    transpose x1, local copies, waits for them, and re-layouts, shards(): x = spectra.transpose(2, 0, 1, 3).reshape(-1, FREQ)  0.95 us

profile of v3, /device:TPU:0, one launch (start us, length us, event | category | flops | bytes accessed | tf_op | source)
XLA Modules:
  0.0 39.0 jit_solution(13375596813054560814)
XLA Ops:
  0.7 0.9 %copy.6 = bf16[2,2,8,2048]{3,2,1,0:T(8,128)(2,1)S(1)} copy(bf16[2,2,8,2048]{3,0,2,1:T(2,128)(2,1)} %bitcast.8) | data formatting | bytes 262144 | tf_op jit(solution)/shard_map/transpose | solution.py:389
  1.6 0.0 copy-start.1
  1.6 0.7 %copy-done.1 = s32[16,2]{0,1:T(2,128)S(1)} copy-done((s32[16,2]{0,1:T(2,128)S(1)}, s32[16,2]{0,1:T(2,128)}, u32[]{:S(2)}) %copy-start.1) | copy-done | bytes 152
  2.3 0.0 copy-start.2
  2.3 0.7 %copy-done.2 = s32[16,2]{0,1:T(2,128)S(1)} copy-done((s32[16,2]{0,1:T(2,128)S(1)}, s32[16,2]{0,1:T(2,128)}, u32[]{:S(2)}) %copy-start.2) | copy-done | bytes 152
  3.0 30.0 %shard_map.55.coefs = f32[8,256,512]{2,1,0:T(8,128)} custom-call(s32[1]{0:T(128)S(6)} %copy.7.count_ref, bf16[32,2048]{1,0:T(8,128)(2,1)S(1)} %bitcast.5, s32[2,16]{1,0:T(2,128)S(1)} %bitcast.6, s32[2,16]{1,0:T(2,128)S(1)} %bitcast.7, bf16[8,512,512]{2,1,0:T(8,128)(2,1)} %constant.2.clone.basis_ref), custom_call_target="tpu_custom_call" | custom-call | tf_op jit(solution)/shard_map/pallas_call | solution.py:303
  33.0 0.0 copy-start
  33.0 2.2 %copy-done = f32[8,256,512]{2,1,0:T(8,128)S(1)} copy-done((f32[8,256,512]{2,1,0:T(8,128)S(1)}, f32[8,256,512]{2,1,0:T(8,128)}, u32[]{:S(2)}) %copy-start) | copy-done | bytes 4194328
  35.2 3.8 %shard_map.56 = f32[256,4096]{1,0:T(8,128)} custom-call(f32[8,256,512]{2,1,0:T(8,128)S(1)} %copy-done), custom_call_target="tpu_custom_call" | custom-call | tf_op jit(solution)/shard_map/pallas_call | solution.py:376
Async XLA Ops:
  1.6 0.7 %copy-start.1 = (s32[16,2]{0,1:T(2,128)S(1)}, s32[16,2]{0,1:T(2,128)}, u32[]{:S(2)}) copy-start(s32[16,2]{0,1:T(2,128)} %param.7) | copy-start | bytes 388
  2.3 0.7 %copy-start.2 = (s32[16,2]{0,1:T(2,128)S(1)}, s32[16,2]{0,1:T(2,128)}, u32[]{:S(2)}) copy-start(s32[16,2]{0,1:T(2,128)} %param.6) | copy-start | bytes 388
  33.0 2.2 %copy-start = (f32[8,256,512]{2,1,0:T(8,128)S(1)}, f32[8,256,512]{2,1,0:T(8,128)}, u32[]{:S(2)}) copy-start(f32[8,256,512]{2,1,0:T(8,128)} %shard_map.55.coefs) | copy-start | bytes 12582916

commit v4 on v3

--- a/solution.py
+++ b/solution.py
@@ -104,8 +104,7 @@
     n,
     count_ref,
     x_ref,
-    dest_ref,
-    blocks_ref,
+    pairs_ref,
     basis_ref,
     coef_ref,
     all_ref,
@@ -153,12 +152,12 @@
     for fetch in fetches:
         fetch.start()
 
-    slots = dest_ref.shape[1]
+    slots = pairs_ref.shape[1]
     used = lax.broadcasted_iota(jnp.int32, (1, slots), 1) < count_ref[0]
     lists[...] = jnp.full(lists.shape, -1.0, jnp.float32)
-    lists[0:1, 0:slots] = jnp.where(used, dest_ref[0:1, :], -1).astype(jnp.float32)
-    lists[1:2, 0:slots] = dest_ref[1:2, :].astype(jnp.float32)
-    lists[2:4, 0:slots] = (blocks_ref[...] + 1).astype(jnp.float32)
+    lists[0:1, 0:slots] = jnp.where(used, pairs_ref[0:1, :], -1).astype(jnp.float32)
+    lists[1:2, 0:slots] = pairs_ref[1:2, :].astype(jnp.float32)
+    lists[2:4, 0:slots] = (pairs_ref[2:4, :] + 1).astype(jnp.float32)
     piece[RADIX] = lists[...].astype(jnp.bfloat16)
     rows = x_ref.shape[0]
     half = rows // 2
@@ -275,15 +274,14 @@
             y_step(t - 1, 1)
     y_step(nz, 0)
     z_step(nz - 1, 1)
+    y_step(nz - 1, 1)
     own.wait()
     for fetch in fetches:
         fetch.wait()
     c_wait(0)
     fill_pick(n, slots, all_ref, pick)
-    cross_steps(6, 8)
-    y_step(nz - 1, 1)
     y_step(nz, 1)
-    cross_steps(4, 6)
+    cross_steps(4, 8)
     c_wait(1)
     cross_steps(0, 4)
     for condition, copy in copies:
@@ -291,19 +289,19 @@
 
 
 def limit(rows):
-    return 60 * 1024 * 1024 - rows * LAGS * 8
-
-
-def gather(n, count, x, dest, blocks, basis):
+    return 56 * 1024 * 1024 - rows * LAGS * 8
+
+
+def gather(n, count, x, pairs, basis):
     half = x.shape[0] // 2
-    rows = dest.shape[1] * CH * CH
+    rows = pairs.shape[1] * CH * CH
     shape = (RADIX + 1, half, 2 * BINS)
     vmem = pl.BlockSpec(memory_space=pltpu.VMEM)
     hbm = pl.BlockSpec(memory_space=pltpu.HBM)
     return pl.pallas_call(
         functools.partial(gather_kernel, n),
         out_shape=jax.ShapeDtypeStruct((PAIRS, rows, 2 * SPAN), jnp.float32),
-        in_specs=[pl.BlockSpec(memory_space=pltpu.SMEM), vmem, vmem, vmem, hbm],
+        in_specs=[pl.BlockSpec(memory_space=pltpu.SMEM), vmem, vmem, hbm],
         out_specs=vmem,
         scratch_shapes=[
             pltpu.VMEM((n,) + shape, jnp.bfloat16),
@@ -319,7 +317,7 @@
         compiler_params=pltpu.CompilerParams(
             collective_id=0, has_side_effects=True, vmem_limit_bytes=limit(rows)
         ),
-    )(count, x, dest, blocks, basis)
+    )(count, x, pairs, basis)
 
 
 def transform(coef, put):
@@ -387,7 +385,8 @@
     slots = pair_dest.shape[0]
     n = lax.axis_size("chan")
     x = spectra.transpose(2, 0, 1, 3).reshape(-1, FREQ)
-    coefs = gather(n, pair_count, x, pair_dest.T, pair_blocks.T, jnp.asarray(basis))
+    pairs = jnp.concatenate([pair_dest.T, pair_blocks.T])
+    coefs = gather(n, pair_count, x, pairs, jnp.asarray(basis))
     out = stack(coefs)
     return out.reshape(slots, CH * CH, LAGS)
 

time: 39.2 us -> 35.8 us (0.913)
  local copies, waits for them, and re-layouts: 4.48 us -> 0.95 us
  other arithmetic: 0 us -> 0.7 us
  Pallas kernels: 33.8 us -> 33.3 us
    unnamed x6 -> x0, local copies, waits for them, and re-layouts: 3.53 us -> none
    concatenate x0 -> x1, other arithmetic: none -> 0.7 us  [shards(): pairs = jnp.concatenate([pair_dest.T, pair_blocks.T])]
    pallas_call x1, Pallas kernels: 30 us -> 29.5 us  [gather(): pl.pallas_call(functools.partial(gather_kernel, n), out_shape=jax.ShapeDt...]
where the time goes in v4:
time: 35.8 us; the launch traced here: 35.6 us
  Pallas kernels  33.3 us (93%)
  local copies, waits for them, and re-layouts  0.95 us (3%)
  other arithmetic  0.7 us (2%)
  between operations  0.66 us (2%)
    pallas_call x1, Pallas kernels, gather(): pl.pallas_call(functools.partial(gather_kernel, n), out_shape=jax.ShapeDt...  29.5 us
    pallas_call x1, Pallas kernels, stack(): pl.pallas_call(functools.partial(stack_kernel, chunk), out_shape=jax.Shap...  3.84 us
    transpose x1, local copies, waits for them, and re-layouts, shards(): x = spectra.transpose(2, 0, 1, 3).reshape(-1, FREQ)  0.95 us

profile of v4, /device:TPU:0, one launch (start us, length us, event | category | flops | bytes accessed | tf_op | source)
XLA Modules:
  0.0 35.6 jit_solution(14788381835432603060)
XLA Ops:
  0.7 0.7 %pad_add_fusion.pairs_ref = s32[4,16]{1,0:T(4,128)S(1)} fusion(s32[2,16]{1,0:T(2,128)} %bitcast.7, s32[2,16]{1,0:T(2,128)} %bitcast.8), kind=kLoop, calls=%fused_computation | loop fusion | flops 64 | bytes 512 | tf_op jit(solution)/shard_map/concatenate | solution.py:388
  1.4 0.9 %copy.6 = bf16[2,2,8,2048]{3,2,1,0:T(8,128)(2,1)S(1)} copy(bf16[2,2,8,2048]{3,0,2,1:T(2,128)(2,1)} %bitcast.6) | data formatting | bytes 262144 | tf_op jit(solution)/shard_map/transpose | solution.py:387
  2.3 29.5 %shard_map.55.coefs = f32[8,256,512]{2,1,0:T(8,128)S(1)} custom-call(s32[1]{0:T(128)S(6)} %copy.7.count_ref, bf16[32,2048]{1,0:T(8,128)(2,1)S(1)} %bitcast.5, s32[4,16]{1,0:T(4,128)S(1)} %pad_add_fusion.pairs_ref, bf16[8,512,512]{2,1,0:T(8,128)(2,1)} %constant.2.clone.basis_ref), custom_call_target="tpu_custom_call" | custom-call | tf_op jit(solution)/shard_map/pallas_call | solution.py:301
  31.8 3.8 %shard_map.56 = f32[256,4096]{1,0:T(8,128)} custom-call(f32[8,256,512]{2,1,0:T(8,128)S(1)} %shard_map.55.coefs), custom_call_target="tpu_custom_call" | custom-call | tf_op jit(solution)/shard_map/pallas_call | solution.py:374

commit v5 on v4

--- a/solution.py
+++ b/solution.py
@@ -261,10 +261,11 @@
 
     def cross_steps(low, high):
         def body(q, carry):
-            cross_step(rows, q, all_ref, pick, basis, coef_ref)
+            for k in range(2):
+                cross_step(rows, 2 * q + k, all_ref, pick, basis, coef_ref)
             return carry
 
-        lax.fori_loop(low, high, body, 0)
+        lax.fori_loop(low // 2, high // 2, body, 0)
 
     for t in range(1, nz):
         z_step(t, 0)
@@ -360,12 +361,13 @@
 
             def put(na, value):
                 col = na * SPAN + h * 128
-                out_ref[pl.ds(pl.multiple_of(i * 8, 8), 8), col : col + 128] = value
+                out_ref[i * 8 : i * 8 + 8, col : col + 128] = value
 
             transform(coef, put)
         return carry
 
-    lax.fori_loop(0, chunk // 8, body, 0)
+    for i in range(chunk // 8):
+        body(i, 0)
 
 
 def stack(coefs):

time: 35.8 us -> 35.1 us (0.980)
  Pallas kernels: 33.3 us -> 32.6 us
    pallas_call x1, Pallas kernels: 29.5 us -> 28.9 us  [gather(): pl.pallas_call(functools.partial(gather_kernel, n), out_shape=jax.ShapeDt...]
where the time goes in v5:
time: 35.1 us; the launch traced here: 35 us
  Pallas kernels  32.6 us (93%)
  local copies, waits for them, and re-layouts  0.95 us (3%)
  other arithmetic  0.7 us (2%)
  between operations  0.66 us (2%)
    pallas_call x1, Pallas kernels, gather(): pl.pallas_call(functools.partial(gather_kernel, n), out_shape=jax.ShapeDt...  28.9 us
    pallas_call x1, Pallas kernels, stack(): pl.pallas_call(functools.partial(stack_kernel, chunk), out_shape=jax.Shap...  3.75 us
    transpose x1, local copies, waits for them, and re-layouts, shards(): x = spectra.transpose(2, 0, 1, 3).reshape(-1, FREQ)  0.95 us
    concatenate x1, other arithmetic, shards(): pairs = jnp.concatenate([pair_dest.T, pair_blocks.T])  0.7 us

profile of v5, /device:TPU:0, one launch (start us, length us, event | category | flops | bytes accessed | tf_op | source)
XLA Modules:
  0.0 35.0 jit_solution(17314402435964142489)
XLA Ops:
  0.7 0.7 %pad_add_fusion.pairs_ref = s32[4,16]{1,0:T(4,128)S(1)} fusion(s32[2,16]{1,0:T(2,128)} %bitcast.7, s32[2,16]{1,0:T(2,128)} %bitcast.8), kind=kLoop, calls=%fused_computation | loop fusion | flops 64 | bytes 512 | tf_op jit(solution)/shard_map/concatenate | solution.py:390
  1.4 0.9 %copy.6 = bf16[2,2,8,2048]{3,2,1,0:T(8,128)(2,1)S(1)} copy(bf16[2,2,8,2048]{3,0,2,1:T(2,128)(2,1)} %bitcast.6) | data formatting | bytes 262144 | tf_op jit(solution)/shard_map/transpose | solution.py:389
  2.3 28.9 %shard_map.55.coefs = f32[8,256,512]{2,1,0:T(8,128)S(1)} custom-call(s32[1]{0:T(128)S(6)} %copy.7.count_ref, bf16[32,2048]{1,0:T(8,128)(2,1)S(1)} %bitcast.5, s32[4,16]{1,0:T(4,128)S(1)} %pad_add_fusion.pairs_ref, bf16[8,512,512]{2,1,0:T(8,128)(2,1)} %constant.2.clone.basis_ref), custom_call_target="tpu_custom_call" | custom-call | tf_op jit(solution)/shard_map/pallas_call | solution.py:302
  31.2 3.8 %shard_map.56 = f32[256,4096]{1,0:T(8,128)} custom-call(f32[8,256,512]{2,1,0:T(8,128)S(1)} %shard_map.55.coefs), custom_call_target="tpu_custom_call" | custom-call | tf_op jit(solution)/shard_map/pallas_call | solution.py:376
